TPU v7x, 32 devices: a whole 2x2x4 slice. The times are simulated.
32 devices in a mesh: pool: 2 (over x), pencil: 8 (over z, y), tgroup: 2 (over core).
Axes of the slice: x: 2, y: 2, z: 4, core: 2. Of those that a mesh axis runs over, the one named last changes fastest.
Arguments:
- dpsi: float32 [2, 4, 196608], P(None, 'pool', ('pencil', 'tgroup')), parts along dimension 1, may hold values from -6 to 6
- stick_cols: int32 [3072], replicated, may hold values from 0 to 16383, as said below
- pw_z: int32 [3072, 64], P('pencil'), may hold values from 0 to 127, as said below
- v_local: float32 [128, 16384], P('pencil'), may hold values from -6 to 6
- dv: float32 [128, 16384], P('pencil'), may hold values from -6 to 6
Outputs:
- h_dpsi: float32 [2, 4, 196608], P(None, 'pool', ('pencil', 'tgroup')), parts along dimension 1
There are 2 independent parts, one for each index of `pool`. A program takes and returns all parts, laid end to end along the dimension named above; an argument that names none is the same for every part. Nothing has to cross between parts.
Inputs may be any that keep to these rules, and one draw needn't show every extreme that they name: `stick_cols`: the 3072 values are distinct. `pw_z`: the 64 values of each row are distinct.
All inputs are finite; a program needn't handle non-finite values.
Results may differ from a plain program's by a relative error of at most 0.00007.
Values sent between devices are 32-bit elements; how exact they have to be, the bound alone decides.
A program may use at most 128 MiB of HBM per device.

v0:
```python
from functools import partial
import math

import jax
import jax.numpy as jnp
import ml_dtypes
import numpy as np
from jax import lax
from jax.experimental import pallas as pl
from jax.experimental.pallas import tpu as pltpu
from jax.sharding import PartitionSpec as P

F32 = jnp.float32
BF16 = jnp.bfloat16
LANES = 128
GROUP = 32


def halves(table):
    hi = table.astype(ml_dtypes.bfloat16)
    lo = (table - hi.astype(np.float64)).astype(ml_dtypes.bfloat16)
    return hi, lo


def split(value):
    hi = value.astype(BF16)
    lo = (value - hi.astype(F32)).astype(BF16)
    return hi, lo


def dot3(left, right, dims=((1,), (0,))):
    mul = lambda a, b: lax.dot_general(a, b, (dims, ((), ())), preferred_element_type=F32)
    return mul(left[0], right[0]) + (mul(left[0], right[1]) + mul(left[1], right[0]))


def waves(length):
    k = np.arange(length)
    angle = (k[:, None] * k[None, :] % length) * (2.0 * math.pi / length)
    return np.cos(angle) / math.sqrt(length), np.sin(angle) / math.sqrt(length)


def depth_table(length, devices):
    cos, sin = waves(length)
    planes = length // devices
    whole = np.stack([np.stack([cos, -sin], 1), np.stack([sin, cos], 1)])
    whole = whole.reshape(2, devices, planes, 2 * length)
    return whole.transpose(1, 0, 2, 3).reshape(2 * length, 2 * length)


def row_tables(length):
    cos, sin = waves(length)
    return np.concatenate([cos, sin]), np.concatenate([cos, -sin])


def column_table(length, slots):
    cos, sin = waves(length)
    whole = np.stack([np.stack([cos, -sin], 1), np.stack([sin, cos], 1)])
    whole = whole.reshape(2, length, 2, slots, length // slots)
    return whole.transpose(0, 1, 4, 2, 3).reshape(2 * length, 2 * length)


class Peers:
    def __init__(self):
        self.cores = lax.axis_size("tgroup")
        self.count = lax.axis_size("pencil") * self.cores
        self.me = lax.axis_index("pencil") * self.cores + lax.axis_index("tgroup")
        self.barrier = pltpu.get_barrier_semaphore()

    def at(self, step):
        return lax.rem(self.me + step, self.count)

    def step(self, turn):
        away = lax.div(turn, 2)
        return self.count // 2 + jnp.where(lax.rem(turn, 2) == 0, away, -away)

    def name(self, device):
        return {"pencil": lax.div(device, self.cores), "tgroup": lax.rem(device, self.cores)}

    def greet(self):
        @pl.loop(1, self.count)
        def _(step):
            pl.semaphore_signal(
                self.barrier,
                inc=1,
                device_id=self.name(self.at(step)),
                device_id_type=pl.DeviceIdType.MESH,
            )

    def met(self):
        pl.semaphore_wait(self.barrier, self.count - 1)

    def copy(self, step, source, target, sent, got):
        peer = self.at(step)
        return pltpu.make_async_remote_copy(
            src_ref=source.at[peer],
            dst_ref=target.at[self.me],
            send_sem=sent.at[step],
            recv_sem=got.at[step],
            device_id=self.name(peer),
            device_id_type=pl.DeviceIdType.MESH,
        )

    def settle(self, source, target, sent, got):
        @pl.loop(1, self.count)
        def _(step):
            self.copy(step, source, target, sent, got).wait()


def depth_up(
    coeff_ref,
    pw_ref,
    table_ref,
    out_ref,
    ready,
    coeff,
    inverse,
    column,
    sent,
    got,
):
    peers = Peers()
    peers.greet()
    bands = coeff_ref.shape[1]
    _, _, rows, width = coeff.shape
    devices, part_rows, _ = out_ref.shape
    zpw, own = pw_ref.shape
    length = inverse.shape[1]
    for part in range(2):
        for band in range(bands):
            for row in range(rows):
                coeff[part, band, row : row + 1] = coeff_ref[
                    part, band : band + 1, row * width : (row + 1) * width
                ]
    z = lax.broadcasted_iota(jnp.int32, (length, LANES), 0)
    for tile in range(own // LANES + (own % LANES > 0)):
        lanes = slice(tile * LANES, min((tile + 1) * LANES, own))
        source = jnp.full((length, LANES), -1, jnp.int32)
        for k in range(zpw):
            row = pw_ref[k : k + 1, lanes]
            if row.shape[1] < LANES:
                row = jnp.concatenate(
                    [row, jnp.full((1, LANES - row.shape[1]), -1, jnp.int32)], axis=1
                )
            source = jnp.where(row == z, k, source)
        inverse[tile * LANES : (tile + 1) * LANES] = source.T
    for parity in range(2):
        source = inverse[pl.ds(parity, rows, stride=2), :]
        found = source >= 0
        source = jnp.maximum(source, 0) + parity * zpw
        for band in range(bands):
            places = pl.ds(band * own + parity, rows, stride=2)
            for part in range(2):
                taken = jnp.take_along_axis(
                    coeff[part, band], source, axis=1, mode="promise_in_bounds"
                )
                column[part, places, :] = jnp.where(found, taken, 0.0)
    value = jnp.concatenate([column[0], column[1]], axis=1)
    field = dot3((table_ref[0], table_ref[1]), split(value), ((1,), (1,)))
    for device in range(devices):
        ready[device] = field[device * part_rows : (device + 1) * part_rows]
    peers.met()

    @pl.loop(1, devices)
    def _(turn):
        peers.copy(peers.step(turn), ready, out_ref, sent, got).start()

    out_ref[peers.me] = ready[peers.me]
    peers.settle(ready, out_ref, sent, got)


def turn(value):
    half = value.shape[0] // 2
    return jnp.concatenate([-value[half:], value[:half]], axis=0)


def row_product(pair, table):
    length = table.shape[1] // 2
    mul = partial(jnp.dot, preferred_element_type=F32)
    both = mul(pair[0], table[...])
    return both[:, :length] + (both[:, length:] + mul(pair[1], table[:, :length]))


def plane_kernel(
    bands,
    cols_ref,
    field_ref,
    local_ref,
    change_ref,
    up,
    down,
    column_hi,
    column_lo,
    back_hi,
    back_lo,
    out_ref,
    flat,
    sticks,
    grid,
    other,
    weights,
):
    devices, part_rows, block = field_ref.shape
    planes = part_rows // 2
    own = block // bands
    length = math.isqrt(local_ref.shape[1])
    bz = bands * planes
    slots = LANES // (2 * bz)
    inner = length // slots
    group_rows = inner * length
    batch = math.gcd(inner, 8)
    total = devices * own
    shift = group_rows.bit_length() - 1

    core = lax.axis_index("tgroup")
    for x in range(length):
        lanes = slice(x * length, (x + 1) * length)
        whole = local_ref[:, lanes] + change_ref[:, lanes]
        mine = whole[:planes]
        for rank in range(1, lax.axis_size("tgroup")):
            mine = jnp.where(core == rank, whole[rank * planes : (rank + 1) * planes], mine)
        weights[x * planes : (x + 1) * planes] = mine
    grid[...] = jnp.zeros_like(grid)
    for device in range(devices):
        for part in range(2):
            for band in range(bands):
                flat[
                    (part * bands + band) * planes : (part * bands + band + 1) * planes,
                    device * own : (device + 1) * own,
                ] = field_ref[
                    device, part * planes : (part + 1) * planes, band * own : (band + 1) * own
                ]
    for tile in range(total // LANES):
        value = flat[:, tile * LANES : (tile + 1) * LANES]
        value = jnp.concatenate([value[:bz]] * slots + [value[bz:]] * slots, axis=0)
        sticks[tile * LANES : (tile + 1) * LANES] = value.T

    lane = lax.broadcasted_iota(jnp.int32, (1, LANES), 1)
    slot_of_lane = lane // bz % slots

    @pl.loop(0, total // GROUP)
    def _(step):
        base = pl.multiple_of(step * GROUP, GROUP)
        cols = [cols_ref[base + i] for i in range(GROUP)]
        rows = [col & (group_rows - 1) for col in cols]
        masks = [slot_of_lane == lax.shift_right_logical(col, shift) for col in cols]
        values = [sticks[pl.ds(base + i, 1), :] for i in range(GROUP)]
        for value, row, mask in zip(values, rows, masks):
            pltpu.store(grid.at[pl.ds(row, 1), :], value, mask=mask)

    @pl.loop(0, inner // batch)
    def _(step):
        whole = pl.ds(pl.multiple_of(step * batch * length, batch * length), batch * length)
        his, los = [], []
        for i in range(batch):
            start = pl.multiple_of((step * batch + i) * length, length)
            hi, lo = split(grid[pl.ds(start, length), :].T)
            his.append(jnp.concatenate([hi, turn(hi)], axis=1))
            los.append(jnp.concatenate([lo, turn(lo)], axis=1))
        pair = (jnp.concatenate(his, axis=0), jnp.concatenate(los, axis=0))
        other[whole, :] = row_product(pair, up)

    for z in range(planes):
        picks = [pl.ds(band * planes + z, 2 * length, stride=bz) for band in range(bands)]
        value = jnp.concatenate([other[pick, :] for pick in picks], axis=1)
        value = dot3((column_hi[...], column_lo[...]), split(value))
        weight = weights[pl.ds(z, length, stride=planes), :]
        weight = jnp.concatenate([weight] * 2, axis=0)
        weight = jnp.concatenate([weight] * bands, axis=1)
        value = dot3((back_hi[...], back_lo[...]), split(value * weight))
        for band, pick in enumerate(picks):
            grid[pick, :] = value[:, band * length : (band + 1) * length]

    @pl.loop(0, inner // batch)
    def _(step):
        his, los = [], []
        starts = [pl.multiple_of((step * batch + i) * length, length) for i in range(batch)]
        for start in starts:
            hi, lo = split(grid[pl.ds(start, length), :])
            his.append(jnp.concatenate([hi, turn(hi)], axis=1))
            los.append(jnp.concatenate([lo, turn(lo)], axis=1))
        pair = (jnp.concatenate(his, axis=0), jnp.concatenate(los, axis=0))
        value = row_product(pair, down)
        for i, start in enumerate(starts):
            out_ref[pl.ds(start, length), :] = value[i * length : (i + 1) * length].T


def depth_down(
    cols_ref,
    slot_ref,
    grid_ref,
    pw_ref,
    table_ref,
    out_ref,
    ready,
    field,
    sticks,
    flat,
    column,
    sent,
    got,
):
    peers = Peers()
    peers.greet()
    _, bands, rows, width = out_ref.shape
    devices, part_rows, _ = ready.shape
    planes = part_rows // 2
    own = 2 * rows
    length = devices * planes
    bz = bands * planes
    slots = LANES // (2 * bz)
    half = slots * bz
    group_rows = grid_ref.shape[0]
    shift = group_rows.bit_length() - 1
    group = math.gcd(own, GROUP)

    def gather(device):
        @pl.loop(0, own // group)
        def _(chunk):
            start = pl.multiple_of(chunk * group, group)
            first = device * own + start
            cols = [cols_ref[first + i] for i in range(group)]
            values = [grid_ref[pl.ds(col & (group_rows - 1), 1), :] for col in cols]
            for i, value in enumerate(values):
                sticks[pl.ds(start + i, 1), :] = value

        slot_of = lax.shift_right_logical(slot_ref[device], shift)

        tiles = []
        for tile in range(sticks.shape[0] // LANES):
            value = sticks[tile * LANES : (tile + 1) * LANES].T
            here = slot_of[:, tile * LANES : (tile + 1) * LANES]
            sums = []
            for part in range(2):
                total = value[part * half : part * half + bz]
                for slot in range(1, slots):
                    start = part * half + slot * bz
                    total = jnp.where(here == slot, value[start : start + bz], total)
                sums.append(total)
            tiles.append(jnp.concatenate(sums, axis=0))
        value = jnp.concatenate(tiles, axis=1)[:, :own]
        for part in range(2):
            for band in range(bands):
                start = (part * bands + band) * planes
                ready[
                    device, part * planes : (part + 1) * planes, band * own : (band + 1) * own
                ] = value[start : start + planes]

    sticks[...] = jnp.zeros_like(sticks)
    gather(peers.at(peers.step(1)))
    peers.met()
    peers.copy(peers.step(1), ready, field, sent, got).start()

    @pl.loop(2, devices)
    def _(turn):
        step = peers.step(turn)
        gather(peers.at(step))
        peers.copy(step, ready, field, sent, got).start()

    gather(peers.me)
    field[peers.me] = ready[peers.me]
    pw = pw_ref[...]
    first = lax.broadcasted_iota(jnp.int32, (rows, LANES), 1) < width // 2
    peers.settle(ready, field, sent, got)
    for device in range(devices):
        flat[device * part_rows : (device + 1) * part_rows] = field[device]
    value = dot3(split(flat[...]), (table_ref[0], table_ref[1]), ((0,), (0,)))
    column[0] = value[:, :length]
    column[1] = value[:, length:]
    for band in range(bands):
        for part in range(2):
            taken = []
            for parity in range(2):
                piece = column[part, pl.ds(band * own + parity, rows, stride=2), :]
                taken.append(
                    jnp.take_along_axis(piece, pw, axis=1, mode="promise_in_bounds")
                )
            out_ref[part, band] = jnp.where(first, taken[0], taken[1])


VM = pl.BlockSpec(memory_space=pltpu.VMEM)
SM = pl.BlockSpec(memory_space=pltpu.SMEM)
params = partial(pltpu.CompilerParams, vmem_limit_bytes=40 * 1024 * 1024)


def local(dpsi, stick_cols, pw_z, v_local, dv):
    devices = lax.axis_size("pencil") * lax.axis_size("tgroup")
    cores = lax.axis_size("tgroup")
    core = lax.axis_index("tgroup")
    length = math.isqrt(v_local.shape[1])
    planes = v_local.shape[0] // cores
    own = pw_z.shape[0] // cores
    zpw = pw_z.shape[1]
    bands = dpsi.shape[1]
    pairs = own // 2
    bz = bands * planes
    slots = LANES // (2 * bz)

    rows = lax.dynamic_slice_in_dim(pw_z, core * own, own, 0).reshape(pairs, 2 * zpw)
    coeff = (2, bands, pairs, 2 * zpw)
    by_wave = lax.dynamic_slice_in_dim(pw_z.T, core * own, own, 1)

    depth = jnp.asarray(np.stack(halves(depth_table(length, devices))))
    up, down = [jnp.asarray(np.concatenate(halves(table), axis=1)) for table in row_tables(length)]
    column = column_table(length, slots)
    back = [jnp.asarray(half) for half in halves(np.ascontiguousarray(column.T))]
    column = [jnp.asarray(half) for half in halves(column)]

    slot_cols = jnp.pad(stick_cols.reshape(devices, 1, own), ((0, 0), (0, 0), (0, -own % LANES)))
    block = (devices, 2 * planes, bands * own)
    in_slots = length // slots * length
    padded = -(-own // LANES) * LANES
    cost = pl.CostEstimate(
        flops=0, bytes_accessed=100 * math.prod(block) * 4, transcendentals=0
    )
    field = pl.pallas_call(
        depth_up,
        out_shape=jax.ShapeDtypeStruct(block, F32),
        in_specs=[VM] * 3,
        out_specs=VM,
        scratch_shapes=[
            pltpu.VMEM(block, F32),
            pltpu.VMEM(coeff, F32),
            pltpu.VMEM((padded, length), jnp.int32),
            pltpu.VMEM((2, bands * own, length), F32),
            pltpu.SemaphoreType.DMA((devices,)),
            pltpu.SemaphoreType.DMA((devices,)),
        ],
        cost_estimate=cost,
        compiler_params=params(collective_id=0, has_side_effects=True),
    )(dpsi, by_wave, depth)
    grid = pl.pallas_call(
        partial(plane_kernel, bands),
        out_shape=jax.ShapeDtypeStruct((in_slots, LANES), F32),
        in_specs=[SM] + [VM] * 9,
        out_specs=VM,
        scratch_shapes=[
            pltpu.VMEM((2 * bz, devices * own), F32),
            pltpu.VMEM((devices * own, LANES), F32),
            pltpu.VMEM((in_slots, LANES), F32),
            pltpu.VMEM((in_slots, LANES), F32),
            pltpu.VMEM((length * planes, length), F32),
        ],
        cost_estimate=cost,
        compiler_params=params(),
    )(stick_cols, field, v_local, dv, up, down, *column, *back)
    output = pl.pallas_call(
        depth_down,
        out_shape=jax.ShapeDtypeStruct(coeff, F32),
        in_specs=[SM] + [VM] * 4,
        out_specs=VM,
        scratch_shapes=[
            pltpu.VMEM(block, F32),
            pltpu.VMEM(block, F32),
            pltpu.VMEM((padded, LANES), F32),
            pltpu.VMEM((2 * length, bands * own), F32),
            pltpu.VMEM((2, bands * own, length), F32),
            pltpu.SemaphoreType.DMA((devices,)),
            pltpu.SemaphoreType.DMA((devices,)),
        ],
        cost_estimate=cost,
        compiler_params=params(collective_id=1, has_side_effects=True),
    )(stick_cols, slot_cols, grid, rows, depth)
    return output.reshape(dpsi.shape)


def solution(mesh):
    in_specs = (
        P(None, "pool", ("pencil", "tgroup")),
        P(),
        P("pencil", None),
        P("pencil", None),
        P("pencil", None),
    )
    out_specs = P(None, "pool", ("pencil", "tgroup"))
    return jax.shard_map(local, mesh=mesh, in_specs=in_specs, out_specs=out_specs, check_vma=False)
```

profile of v0, /device:TPU:0, one launch (start us, length us, event | category | flops | bytes accessed | tf_op | source)
XLA Modules:
  0.0 54.9 jit_solution(6571934592692726299)
XLA Ops:
  0.0 0.9 %copy-done = s32[384,64]{0,1:T(8,128)S(1)} copy-done((s32[384,64]{0,1:T(8,128)S(1)}, s32[384,64]{0,1:T(8,128)}, u32[]{:S(2)}) %copy-start) | copy-done | bytes 98328
  0.9 0.1 fusion.pw_ref
  1.0 0.0 copy-start.1
  1.0 0.9 %copy-done.1 = bf16[2,256,256]{2,1,0:T(8,128)(2,1)S(1)} copy-done((bf16[2,256,256]{2,1,0:T(8,128)(2,1)S(1)}, bf16[2,256,256]{2,1,0:T(8,128)(2,1)}, u32[]{:S(2)}) %copy-start.1) | copy-done | bytes 262168
  1.9 0.9 %copy-done.5 = f32[2,2,12288]{2,1,0:T(2,128)S(1)} copy-done((f32[2,2,12288]{2,1,0:T(2,128)S(1)}, f32[2,2,12288]{2,1,0:T(2,128)}, u32[]{:S(2)}) %copy-start.5) | copy-done | bytes 196632
  2.9 15.3 %shard_map.118.field_ref = f32[16,16,384]{2,1,0:T(8,128)S(1)} custom-call(f32[2,2,12288]{2,1,0:T(2,128)S(1)} %copy-done.5, s32[64,192]{1,0:T(8,128)S(1)} %fusion.pw_ref, bf16[2,256,256]{2,1,0:T(8,128)(2,1)S(1)} %copy-done.1), custom_call_target="tpu_custom_call" | custom-call | bytes 39321600 | tf_op jit(solution)/shard_map/pallas_call | solution.py:415
  18.2 0.0 copy-start.3
  18.2 1.2 %copy-done.3 = f32[16,16384]{1,0:T(8,128)S(1)} copy-done((f32[16,16384]{1,0:T(8,128)S(1)}, f32[16,16384]{1,0:T(8,128)}, u32[]{:S(2)}) %copy-start.3) | copy-done | bytes 1048600
  19.4 1.2 %copy-done.4 = f32[16,16384]{1,0:T(8,128)S(1)} copy-done((f32[16,16384]{1,0:T(8,128)S(1)}, f32[16,16384]{1,0:T(8,128)}, u32[]{:S(2)}) %copy-start.4) | copy-done | bytes 1048600
  20.7 0.9 %copy-done.6 = bf16[256,256]{1,0:T(8,128)(2,1)S(1)} copy-done((bf16[256,256]{1,0:T(8,128)(2,1)S(1)}, bf16[256,256]{1,0:T(8,128)(2,1)}, u32[]{:S(2)}) %copy-start.6) | copy-done | bytes 131096
  21.6 0.9 %copy-done.7 = bf16[256,256]{1,0:T(8,128)(2,1)S(1)} copy-done((bf16[256,256]{1,0:T(8,128)(2,1)S(1)}, bf16[256,256]{1,0:T(8,128)(2,1)}, u32[]{:S(2)}) %copy-start.7) | copy-done | bytes 131096
  22.5 0.9 %copy-done.8 = bf16[256,256]{1,0:T(8,128)(2,1)S(1)} copy-done((bf16[256,256]{1,0:T(8,128)(2,1)S(1)}, bf16[256,256]{1,0:T(8,128)(2,1)}, u32[]{:S(2)}) %copy-start.8) | copy-done | bytes 131096
  23.4 0.9 %copy-done.9 = bf16[256,256]{1,0:T(8,128)(2,1)S(1)} copy-done((bf16[256,256]{1,0:T(8,128)(2,1)S(1)}, bf16[256,256]{1,0:T(8,128)(2,1)}, u32[]{:S(2)}) %copy-start.9) | copy-done | bytes 131096
  24.3 0.9 %copy-done.10 = bf16[256,256]{1,0:T(8,128)(2,1)S(1)} copy-done((bf16[256,256]{1,0:T(8,128)(2,1)S(1)}, bf16[256,256]{1,0:T(8,128)(2,1)}, u32[]{:S(2)}) %copy-start.10) | copy-done | bytes 131096
  25.2 0.9 %copy-done.11 = bf16[256,256]{1,0:T(8,128)(2,1)S(1)} copy-done((bf16[256,256]{1,0:T(8,128)(2,1)S(1)}, bf16[256,256]{1,0:T(8,128)(2,1)}, u32[]{:S(2)}) %copy-start.11) | copy-done | bytes 131096
  26.1 0.7 %copy-done.12 = s32[3072]{0:T(1024)S(1)} copy-done((s32[3072]{0:T(1024)S(1)}, s32[3072]{0:T(1024)}, u32[]{:S(2)}) %copy-start.12) | copy-done | bytes 12312
  26.8 12.7 %shard_map.119.grid_ref = f32[4096,128]{1,0:T(8,128)S(1)} custom-call(s32[3072]{0:T(1024)S(1)} %copy-done.12, f32[16,16,384]{2,1,0:T(8,128)S(1)} %shard_map.118.field_ref, f32[16,16384]{1,0:T(8,128)S(1)} %copy-done.3, f32[16,16384]{1,0:T(8,128)S(1)} %copy-done.4, bf16[256,256]{1,0:T(8,128)(2,1)S(1)} %copy-done.6, bf16[256,256]{1,0:T(8,128)(2,1)S(1)} %copy-done.7, ...), custom_call_target="tpu_custom_call" | custom-call | bytes 39321600 | tf_op jit(solution)/shard_map/pallas_call | solution.py:431
  39.4 0.1 constant_dynamic-slice_fusion
  39.5 0.1 copy.14
  39.6 0.1 reshape.10.pw_ref
  39.7 0.0 copy-done.13
  39.7 0.1 reshape.9
  39.8 14.3 %shard_map.120 = f32[2,2,96,128]{3,2,1,0:T(8,128)S(1)} custom-call(s32[3072]{0:T(1024)S(1)} %copy-done.13, s32[16,1,256]{2,1,0:T(1,128)S(1)} %pad.4.slot_ref, f32[4096,128]{1,0:T(8,128)S(1)} %shard_map.119.grid_ref, s32[96,128]{1,0:T(8,128)S(1)} %reshape.10.pw_ref, bf16[2,256,256]{2,1,0:T(8,128)(2,1)S(1)} %copy-done.2), custom_call_target="tpu_custom_call" | custom-call | bytes 39321600 | tf_op jit(solution)/shard_map/pallas_call | solution.py:446
  54.1 0.8 %reshape.11 = f32[2,2,12288]{2,1,0:T(2,128)} reshape(f32[2,2,96,128]{3,2,1,0:T(8,128)S(1)} %shard_map.120) | data formatting | bytes 393216 | tf_op jit(solution)/shard_map/reshape | solution.py:463
  (14 shorter events, 0.0 us)
Async XLA Ops:
  0.0 0.9 %copy-start = (s32[384,64]{0,1:T(8,128)S(1)}, s32[384,64]{0,1:T(8,128)}, u32[]{:S(2)}) copy-start(s32[384,64]{0,1:T(8,128)} %param.14) | copy-start | bytes 294916
  1.0 1.0 %copy-start.1 = (bf16[2,256,256]{2,1,0:T(8,128)(2,1)S(1)}, bf16[2,256,256]{2,1,0:T(8,128)(2,1)}, u32[]{:S(2)}) copy-start(bf16[2,256,256]{2,1,0:T(8,128)(2,1)} %constant.24.clone.table_ref) | copy-start | bytes 786436
  1.9 0.9 %copy-start.5 = (f32[2,2,12288]{2,1,0:T(2,128)S(1)}, f32[2,2,12288]{2,1,0:T(2,128)}, u32[]{:S(2)}) copy-start(f32[2,2,12288]{2,1,0:T(2,128)} %coeff_ref.1) | copy-start | bytes 589828
  18.2 1.2 %copy-start.3 = (f32[16,16384]{1,0:T(8,128)S(1)}, f32[16,16384]{1,0:T(8,128)}, u32[]{:S(2)}) copy-start(f32[16,16384]{1,0:T(8,128)} %local_ref.1) | copy-start | bytes 3145732
  19.4 1.2 %copy-start.4 = (f32[16,16384]{1,0:T(8,128)S(1)}, f32[16,16384]{1,0:T(8,128)}, u32[]{:S(2)}) copy-start(f32[16,16384]{1,0:T(8,128)} %change_ref.1) | copy-start | bytes 3145732
  20.7 0.9 %copy-start.6 = (bf16[256,256]{1,0:T(8,128)(2,1)S(1)}, bf16[256,256]{1,0:T(8,128)(2,1)}, u32[]{:S(2)}) copy-start(bf16[256,256]{1,0:T(8,128)(2,1)} %constant.25.clone.up) | copy-start | bytes 393220
  21.6 0.9 %copy-start.7 = (bf16[256,256]{1,0:T(8,128)(2,1)S(1)}, bf16[256,256]{1,0:T(8,128)(2,1)}, u32[]{:S(2)}) copy-start(bf16[256,256]{1,0:T(8,128)(2,1)} %constant.26.clone.down) | copy-start | bytes 393220
  22.5 0.9 %copy-start.8 = (bf16[256,256]{1,0:T(8,128)(2,1)S(1)}, bf16[256,256]{1,0:T(8,128)(2,1)}, u32[]{:S(2)}) copy-start(bf16[256,256]{1,0:T(8,128)(2,1)} %constant.27.clone.back_hi) | copy-start | bytes 393220
  23.4 0.9 %copy-start.9 = (bf16[256,256]{1,0:T(8,128)(2,1)S(1)}, bf16[256,256]{1,0:T(8,128)(2,1)}, u32[]{:S(2)}) copy-start(bf16[256,256]{1,0:T(8,128)(2,1)} %constant.28.clone.back_lo) | copy-start | bytes 393220
  24.3 0.9 %copy-start.10 = (bf16[256,256]{1,0:T(8,128)(2,1)S(1)}, bf16[256,256]{1,0:T(8,128)(2,1)}, u32[]{:S(2)}) copy-start(bf16[256,256]{1,0:T(8,128)(2,1)} %constant.29.clone.column_hi) | copy-start | bytes 393220
  25.2 0.9 %copy-start.11 = (bf16[256,256]{1,0:T(8,128)(2,1)S(1)}, bf16[256,256]{1,0:T(8,128)(2,1)}, u32[]{:S(2)}) copy-start(bf16[256,256]{1,0:T(8,128)(2,1)} %constant.30.clone.column_lo) | copy-start | bytes 393220
  26.1 0.7 %copy-start.12 = (s32[3072]{0:T(1024)S(1)}, s32[3072]{0:T(1024)}, u32[]{:S(2)}) copy-start(s32[3072]{0:T(1024)} %cols_ref.3) | copy-start | bytes 36868
  26.8 12.9 %copy-start.13 = (s32[3072]{0:T(1024)S(1)}, s32[3072]{0:T(1024)}, u32[]{:S(2)}) copy-start(s32[3072]{0:T(1024)} %cols_ref.3) | copy-start | bytes 36868
  26.8 13.0 %copy-start.2 = (bf16[2,256,256]{2,1,0:T(8,128)(2,1)S(1)}, bf16[2,256,256]{2,1,0:T(8,128)(2,1)}, u32[]{:S(2)}) copy-start(bf16[2,256,256]{2,1,0:T(8,128)(2,1)} %constant.24.clone.table_ref) | copy-start | bytes 786436
where the time goes:
time: 55.3 us; the launch traced here: 54.9 us
  Pallas kernels  42.2 us (76%)
  local copies, waits for them, and re-layouts  12.6 us (23%)
    pallas_call x1, Pallas kernels, local(): pl.pallas_call(depth_up, out_shape=jax.ShapeDtypeStruct(block, F32), in_s...  15.3 us
    pallas_call x1, Pallas kernels, local(): pl.pallas_call(depth_down, out_shape=jax.ShapeDtypeStruct(coeff, F32), in...  14.3 us
    pallas_call x1, Pallas kernels, local(): pl.pallas_call(partial(plane_kernel, bands), out_shape=jax.ShapeDtypeStru...  12.7 us
    unnamed x28, local copies, waits for them, and re-layouts  11.3 us

commit v1 on v0

--- a/solution.py
+++ b/solution.py
@@ -184,25 +184,18 @@
     bands,
     cols_ref,
     field_ref,
-    local_ref,
-    change_ref,
-    up,
-    down,
-    column_hi,
-    column_lo,
-    back_hi,
-    back_lo,
+    weight_ref,
+    table_ref,
     out_ref,
     flat,
     sticks,
     grid,
     other,
-    weights,
 ):
     devices, part_rows, block = field_ref.shape
     planes = part_rows // 2
     own = block // bands
-    length = math.isqrt(local_ref.shape[1])
+    length = weight_ref.shape[1]
     bz = bands * planes
     slots = LANES // (2 * bz)
     inner = length // slots
@@ -211,14 +204,6 @@
     total = devices * own
     shift = group_rows.bit_length() - 1
 
-    core = lax.axis_index("tgroup")
-    for x in range(length):
-        lanes = slice(x * length, (x + 1) * length)
-        whole = local_ref[:, lanes] + change_ref[:, lanes]
-        mine = whole[:planes]
-        for rank in range(1, lax.axis_size("tgroup")):
-            mine = jnp.where(core == rank, whole[rank * planes : (rank + 1) * planes], mine)
-        weights[x * planes : (x + 1) * planes] = mine
     grid[...] = jnp.zeros_like(grid)
     for device in range(devices):
         for part in range(2):
@@ -257,16 +242,16 @@
             his.append(jnp.concatenate([hi, turn(hi)], axis=1))
             los.append(jnp.concatenate([lo, turn(lo)], axis=1))
         pair = (jnp.concatenate(his, axis=0), jnp.concatenate(los, axis=0))
-        other[whole, :] = row_product(pair, up)
+        other[whole, :] = row_product(pair, table_ref[2])
 
     for z in range(planes):
         picks = [pl.ds(band * planes + z, 2 * length, stride=bz) for band in range(bands)]
         value = jnp.concatenate([other[pick, :] for pick in picks], axis=1)
-        value = dot3((column_hi[...], column_lo[...]), split(value))
-        weight = weights[pl.ds(z, length, stride=planes), :]
+        value = dot3((table_ref[4], table_ref[5]), split(value))
+        weight = weight_ref[pl.ds(z, length, stride=planes), :]
         weight = jnp.concatenate([weight] * 2, axis=0)
         weight = jnp.concatenate([weight] * bands, axis=1)
-        value = dot3((back_hi[...], back_lo[...]), split(value * weight))
+        value = dot3((table_ref[6], table_ref[7]), split(value * weight))
         for band, pick in enumerate(picks):
             grid[pick, :] = value[:, band * length : (band + 1) * length]
 
@@ -279,7 +264,7 @@
             his.append(jnp.concatenate([hi, turn(hi)], axis=1))
             los.append(jnp.concatenate([lo, turn(lo)], axis=1))
         pair = (jnp.concatenate(his, axis=0), jnp.concatenate(los, axis=0))
-        value = row_product(pair, down)
+        value = row_product(pair, table_ref[3])
         for i, start in enumerate(starts):
             out_ref[pl.ds(start, length), :] = value[i * length : (i + 1) * length].T
 
@@ -399,11 +384,16 @@
     coeff = (2, bands, pairs, 2 * zpw)
     by_wave = lax.dynamic_slice_in_dim(pw_z.T, core * own, own, 1)
 
-    depth = jnp.asarray(np.stack(halves(depth_table(length, devices))))
-    up, down = [jnp.asarray(np.concatenate(halves(table), axis=1)) for table in row_tables(length)]
     column = column_table(length, slots)
-    back = [jnp.asarray(half) for half in halves(np.ascontiguousarray(column.T))]
-    column = [jnp.asarray(half) for half in halves(column)]
+    tables = list(halves(depth_table(length, devices)))
+    tables += [np.concatenate(halves(table), axis=1) for table in row_tables(length)]
+    tables += halves(column) + halves(np.ascontiguousarray(column.T))
+    tables = jnp.asarray(np.stack(tables))
+    potential = lax.dynamic_slice_in_dim(v_local, core * planes, planes, 0)
+    potential = potential + lax.dynamic_slice_in_dim(dv, core * planes, planes, 0)
+    potential = potential.reshape(planes, length, length).transpose(1, 0, 2)
+    by_wave, potential = lax.optimization_barrier((by_wave, potential))
+    potential = potential.reshape(length * planes, length)
 
     slot_cols = jnp.pad(stick_cols.reshape(devices, 1, own), ((0, 0), (0, 0), (0, -own % LANES)))
     block = (devices, 2 * planes, bands * own)
@@ -427,22 +417,21 @@
         ],
         cost_estimate=cost,
         compiler_params=params(collective_id=0, has_side_effects=True),
-    )(dpsi, by_wave, depth)
+    )(dpsi, by_wave, tables)
     grid = pl.pallas_call(
         partial(plane_kernel, bands),
         out_shape=jax.ShapeDtypeStruct((in_slots, LANES), F32),
-        in_specs=[SM] + [VM] * 9,
+        in_specs=[SM] + [VM] * 3,
         out_specs=VM,
         scratch_shapes=[
             pltpu.VMEM((2 * bz, devices * own), F32),
             pltpu.VMEM((devices * own, LANES), F32),
             pltpu.VMEM((in_slots, LANES), F32),
             pltpu.VMEM((in_slots, LANES), F32),
-            pltpu.VMEM((length * planes, length), F32),
         ],
         cost_estimate=cost,
         compiler_params=params(),
-    )(stick_cols, field, v_local, dv, up, down, *column, *back)
+    )(stick_cols, field, potential, tables)
     output = pl.pallas_call(
         depth_down,
         out_shape=jax.ShapeDtypeStruct(coeff, F32),
@@ -459,7 +448,7 @@
         ],
         cost_estimate=cost,
         compiler_params=params(collective_id=1, has_side_effects=True),
-    )(stick_cols, slot_cols, grid, rows, depth)
+    )(stick_cols, slot_cols, grid, rows, tables)
     return output.reshape(dpsi.shape)
 
 

time: 55.3 us -> 46.6 us (0.84)
  local copies, waits for them, and re-layouts: 12.6 us -> 3.06 us
  other arithmetic: 0 us -> 1.26 us
    unnamed x28 -> x8, local copies, waits for them, and re-layouts: 11.3 us -> 1.82 us
    transpose x0 -> x1, other arithmetic: none -> 1.26 us  [local(): potential = potential.reshape(planes, length, length).transpose(1, 0, 2)]
where the time goes in v1:
time: 46.6 us; the launch traced here: 46.5 us
  Pallas kernels  42.1 us (90%)
  local copies, waits for them, and re-layouts  3.06 us (7%)
  other arithmetic  1.26 us (3%)
    pallas_call x1, Pallas kernels, local(): pl.pallas_call(depth_up, out_shape=jax.ShapeDtypeStruct(block, F32), in_s...  15.3 us
    pallas_call x1, Pallas kernels, local(): pl.pallas_call(depth_down, out_shape=jax.ShapeDtypeStruct(coeff, F32), in...  14.3 us
    pallas_call x1, Pallas kernels, local(): pl.pallas_call(partial(plane_kernel, bands), out_shape=jax.ShapeDtypeStru...  12.5 us
    unnamed x8, local copies, waits for them, and re-layouts  1.82 us
    transpose x1, other arithmetic, local(): potential = potential.reshape(planes, length, length).transpose(1, 0, 2)  1.26 us

profile of v1, /device:TPU:0, one launch (start us, length us, event | category | flops | bytes accessed | tf_op | source)
XLA Modules:
  0.0 46.5 jit_solution(9212508778945664541)
XLA Ops:
  0.0 0.0 copy-start
  0.0 0.0 copy-start.1
  0.0 0.0 copy-start.3
  0.0 0.9 %copy-done = s32[384,64]{0,1:T(8,128)S(1)} copy-done((s32[384,64]{0,1:T(8,128)S(1)}, s32[384,64]{0,1:T(8,128)}, u32[]{:S(2)}) %copy-start) | copy-done | bytes 98328
  0.9 0.1 fusion.pw_ref
  1.0 1.3 %add_bitcast_fusion = f32[128,8,128]{2,1,0:T(8,128)S(1)} fusion(f32[16,16384]{1,0:T(8,128)} %param.10, s32[]{:T(128)S(6)} %select_n.9, f32[16,16384]{1,0:T(8,128)} %param.9), kind=kLoop, calls=%fused_computation | loop fusion | flops 131072 | bytes 1572868 | tf_op jit(solution)/shard_map/transpose | solution.py:394
  2.2 0.0 copy-done.1
  2.3 0.0 copy-start.2
  2.3 0.9 %copy-done.2 = f32[2,2,12288]{2,1,0:T(2,128)S(1)} copy-done((f32[2,2,12288]{2,1,0:T(2,128)S(1)}, f32[2,2,12288]{2,1,0:T(2,128)}, u32[]{:S(2)}) %copy-start.2) | copy-done | bytes 196632
  3.2 15.3 %shard_map.64.field_ref = f32[16,16,384]{2,1,0:T(8,128)S(1)} custom-call(f32[2,2,12288]{2,1,0:T(2,128)S(1)} %copy-done.2, s32[64,192]{1,0:T(8,128)S(1)} %fusion.pw_ref, bf16[8,256,256]{2,1,0:T(8,128)(2,1)S(1)} %copy-done.1), custom_call_target="tpu_custom_call" | custom-call | bytes 39321600 | tf_op jit(solution)/shard_map/pallas_call | solution.py:405
  18.5 0.0 copy-done.3
  18.5 12.5 %shard_map.65.grid_ref = f32[4096,128]{1,0:T(8,128)S(1)} custom-call(s32[3072]{0:T(1024)S(1)} %copy-done.3, f32[16,16,384]{2,1,0:T(8,128)S(1)} %shard_map.64.field_ref, f32[1024,128]{1,0:T(8,128)S(1)} %bitcast.9, bf16[8,256,256]{2,1,0:T(8,128)(2,1)S(1)} %copy-done.1), custom_call_target="tpu_custom_call" | custom-call | bytes 39321600 | tf_op jit(solution)/shard_map/pallas_call | solution.py:421
  31.0 0.1 constant_dynamic-slice_fusion
  31.1 0.1 copy.8
  31.2 0.1 reshape.18.pw_ref
  31.3 0.1 reshape.15
  31.4 14.3 %shard_map.66 = f32[2,2,96,128]{3,2,1,0:T(8,128)S(1)} custom-call(s32[3072]{0:T(1024)S(1)} %copy-done.3, s32[16,1,256]{2,1,0:T(1,128)S(1)} %pad.4.slot_ref, f32[4096,128]{1,0:T(8,128)S(1)} %shard_map.65.grid_ref, s32[96,128]{1,0:T(8,128)S(1)} %reshape.18.pw_ref, bf16[8,256,256]{2,1,0:T(8,128)(2,1)S(1)} %copy-done.1), custom_call_target="tpu_custom_call" | custom-call | bytes 39321600 | tf_op jit(solution)/shard_map/pallas_call | solution.py:435
  45.7 0.8 %reshape.19 = f32[2,2,12288]{2,1,0:T(2,128)} reshape(f32[2,2,96,128]{3,2,1,0:T(8,128)S(1)} %shard_map.66) | data formatting | bytes 393216 | tf_op jit(solution)/shard_map/reshape | solution.py:452
  (1 shorter events, 0.0 us)
Async XLA Ops:
  0.0 0.9 %copy-start = (s32[384,64]{0,1:T(8,128)S(1)}, s32[384,64]{0,1:T(8,128)}, u32[]{:S(2)}) copy-start(s32[384,64]{0,1:T(8,128)} %param.8) | copy-start | bytes 294916
  0.0 2.2 %copy-start.1 = (bf16[8,256,256]{2,1,0:T(8,128)(2,1)S(1)}, bf16[8,256,256]{2,1,0:T(8,128)(2,1)}, u32[]{:S(2)}) copy-start(bf16[8,256,256]{2,1,0:T(8,128)(2,1)} %constant.16.clone.table_ref) | copy-start | bytes 3145732
  0.0 18.5 %copy-start.3 = (s32[3072]{0:T(1024)S(1)}, s32[3072]{0:T(1024)}, u32[]{:S(2)}) copy-start(s32[3072]{0:T(1024)} %cols_ref.3) | copy-start | bytes 36868
  2.3 0.9 %copy-start.2 = (f32[2,2,12288]{2,1,0:T(2,128)S(1)}, f32[2,2,12288]{2,1,0:T(2,128)}, u32[]{:S(2)}) copy-start(f32[2,2,12288]{2,1,0:T(2,128)} %coeff_ref.1) | copy-start | bytes 589828

commit v2 on v1

--- a/solution.py
+++ b/solution.py
@@ -127,10 +127,14 @@
     length = inverse.shape[1]
     for part in range(2):
         for band in range(bands):
-            for row in range(rows):
-                coeff[part, band, row : row + 1] = coeff_ref[
-                    part, band : band + 1, row * width : (row + 1) * width
+            for start in range(0, rows, 3 * GROUP // 2):
+                some = range(start, min(start + 3 * GROUP // 2, rows))
+                values = [
+                    coeff_ref[part, band : band + 1, row * width : (row + 1) * width]
+                    for row in some
                 ]
+                for row, value in zip(some, values):
+                    coeff[part, band, row : row + 1] = value
     z = lax.broadcasted_iota(jnp.int32, (length, LANES), 0)
     for tile in range(own // LANES + (own % LANES > 0)):
         lanes = slice(tile * LANES, min((tile + 1) * LANES, own))
@@ -202,35 +206,47 @@
     group_rows = inner * length
     batch = math.gcd(inner, 8)
     total = devices * own
-    shift = group_rows.bit_length() - 1
 
     grid[...] = jnp.zeros_like(grid)
-    for device in range(devices):
-        for part in range(2):
-            for band in range(bands):
-                flat[
-                    (part * bands + band) * planes : (part * bands + band + 1) * planes,
-                    device * own : (device + 1) * own,
-                ] = field_ref[
+    for part in range(2):
+        for band in range(bands):
+            start = (part * bands + band) * planes
+            values = [
+                field_ref[
                     device, part * planes : (part + 1) * planes, band * own : (band + 1) * own
                 ]
-    for tile in range(total // LANES):
-        value = flat[:, tile * LANES : (tile + 1) * LANES]
-        value = jnp.concatenate([value[:bz]] * slots + [value[bz:]] * slots, axis=0)
-        sticks[tile * LANES : (tile + 1) * LANES] = value.T
+                for device in range(devices)
+            ]
+            for device, value in enumerate(values):
+                flat[start : start + planes, device * own : (device + 1) * own] = value
+    for start in range(0, total // LANES, 6):
+        some = range(start, min(start + 6, total // LANES))
+        values = [flat[:, tile * LANES : (tile + 1) * LANES] for tile in some]
+        for tile, value in zip(some, values):
+            value = jnp.concatenate([value[:bz]] * slots + [value[bz:]] * slots, axis=0)
+            sticks[tile * LANES : (tile + 1) * LANES] = value.T
 
     lane = lax.broadcasted_iota(jnp.int32, (1, LANES), 1)
-    slot_of_lane = lane // bz % slots
-
-    @pl.loop(0, total // GROUP)
-    def _(step):
-        base = pl.multiple_of(step * GROUP, GROUP)
-        cols = [cols_ref[base + i] for i in range(GROUP)]
-        rows = [col & (group_rows - 1) for col in cols]
-        masks = [slot_of_lane == lax.shift_right_logical(col, shift) for col in cols]
-        values = [sticks[pl.ds(base + i, 1), :] for i in range(GROUP)]
-        for value, row, mask in zip(values, rows, masks):
-            pltpu.store(grid.at[pl.ds(row, 1), :], value, mask=mask)
+    first_of_lane = (lane // bz % slots) * group_rows
+    group = GROUP // 2
+
+    def fetch(step):
+        base = pl.multiple_of(step * group, group)
+        cols = [cols_ref[base + i] for i in range(group)]
+        return cols, [sticks[pl.ds(base + i, 1), :] for i in range(group)]
+
+    def scatter(cols, values):
+        for col, value in zip(cols, values):
+            spread = jnp.full((1, LANES), col, jnp.int32)
+            mask = (spread & -group_rows) == first_of_lane
+            pltpu.store(grid.at[pl.ds(col & (group_rows - 1), 1), :], value, mask=mask)
+
+    def each(step, held):
+        following = fetch(step)
+        scatter(*held)
+        return following
+
+    scatter(*lax.fori_loop(1, total // group, each, fetch(0)))
 
     @pl.loop(0, inner // batch)
     def _(step):
@@ -244,15 +260,22 @@
         pair = (jnp.concatenate(his, axis=0), jnp.concatenate(los, axis=0))
         other[whole, :] = row_product(pair, table_ref[2])
 
+    def picks(z):
+        return [pl.ds(band * planes + z, 2 * length, stride=bz) for band in range(bands)]
+
+    def planes_of(z):
+        return split(jnp.concatenate([other[pick, :] for pick in picks(z)], axis=1))
+
+    following = planes_of(0)
     for z in range(planes):
-        picks = [pl.ds(band * planes + z, 2 * length, stride=bz) for band in range(bands)]
-        value = jnp.concatenate([other[pick, :] for pick in picks], axis=1)
-        value = dot3((table_ref[4], table_ref[5]), split(value))
+        value = dot3((table_ref[4], table_ref[5]), following)
+        if z + 1 < planes:
+            following = planes_of(z + 1)
         weight = weight_ref[pl.ds(z, length, stride=planes), :]
         weight = jnp.concatenate([weight] * 2, axis=0)
         weight = jnp.concatenate([weight] * bands, axis=1)
         value = dot3((table_ref[6], table_ref[7]), split(value * weight))
-        for band, pick in enumerate(picks):
+        for band, pick in enumerate(picks(z)):
             grid[pick, :] = value[:, band * length : (band + 1) * length]
 
     @pl.loop(0, inner // batch)
@@ -296,17 +319,26 @@
     half = slots * bz
     group_rows = grid_ref.shape[0]
     shift = group_rows.bit_length() - 1
-    group = math.gcd(own, GROUP)
+    group = math.gcd(own, GROUP // 2)
 
     def gather(device):
-        @pl.loop(0, own // group)
-        def _(chunk):
+        def fetch(chunk):
+            first = device * own + chunk * group
+            cols = [cols_ref[first + i] for i in range(group)]
+            return [grid_ref[pl.ds(col & (group_rows - 1), 1), :] for col in cols]
+
+        def put(chunk, values):
             start = pl.multiple_of(chunk * group, group)
-            first = device * own + start
-            cols = [cols_ref[first + i] for i in range(group)]
-            values = [grid_ref[pl.ds(col & (group_rows - 1), 1), :] for col in cols]
             for i, value in enumerate(values):
                 sticks[pl.ds(start + i, 1), :] = value
+
+        def each(chunk, held):
+            following = fetch(chunk)
+            put(chunk - 1, held)
+            return following
+
+        chunks = own // group
+        put(chunks - 1, lax.fori_loop(1, chunks, each, fetch(0)))
 
         slot_of = lax.shift_right_logical(slot_ref[device], shift)
 

time: 46.6 us -> 48.1 us (1.032)
  Pallas kernels: 42.1 us -> 43.6 us
    pallas_call x1, Pallas kernels: 12.5 us -> 13.9 us  [local(): pl.pallas_call(partial(plane_kernel, bands), out_shape=jax.ShapeDtypeStru...]
where the time goes in v2:
time: 48.1 us; the launch traced here: 48 us
  Pallas kernels  43.6 us (91%)
  local copies, waits for them, and re-layouts  3.06 us (6%)
  other arithmetic  1.26 us (3%)
    pallas_call x1, Pallas kernels, local(): pl.pallas_call(depth_up, out_shape=jax.ShapeDtypeStruct(block, F32), in_s...  15.3 us
    pallas_call x1, Pallas kernels, local(): pl.pallas_call(depth_down, out_shape=jax.ShapeDtypeStruct(coeff, F32), in...  14.4 us
    pallas_call x1, Pallas kernels, local(): pl.pallas_call(partial(plane_kernel, bands), out_shape=jax.ShapeDtypeStru...  13.9 us
    unnamed x8, local copies, waits for them, and re-layouts  1.82 us
    transpose x1, other arithmetic, local(): potential = potential.reshape(planes, length, length).transpose(1, 0, 2)  1.26 us

profile of v2, /device:TPU:0, one launch (start us, length us, event | category | flops | bytes accessed | tf_op | source)
XLA Modules:
  0.0 48.0 jit_solution(7632328961144588078)
XLA Ops:
  0.0 0.0 copy-start
  0.0 0.0 copy-start.1
  0.0 0.0 copy-start.3
  0.0 0.9 %copy-done = s32[384,64]{0,1:T(8,128)S(1)} copy-done((s32[384,64]{0,1:T(8,128)S(1)}, s32[384,64]{0,1:T(8,128)}, u32[]{:S(2)}) %copy-start) | copy-done | bytes 98328
  0.9 0.1 fusion.pw_ref
  1.0 1.3 %add_bitcast_fusion = f32[128,8,128]{2,1,0:T(8,128)S(1)} fusion(f32[16,16384]{1,0:T(8,128)} %param.10, s32[]{:T(128)S(6)} %select_n.9, f32[16,16384]{1,0:T(8,128)} %param.9), kind=kLoop, calls=%fused_computation | loop fusion | flops 131072 | bytes 1572868 | tf_op jit(solution)/shard_map/transpose | solution.py:426
  2.2 0.0 copy-done.1
  2.3 0.0 copy-start.2
  2.3 0.9 %copy-done.2 = f32[2,2,12288]{2,1,0:T(2,128)S(1)} copy-done((f32[2,2,12288]{2,1,0:T(2,128)S(1)}, f32[2,2,12288]{2,1,0:T(2,128)}, u32[]{:S(2)}) %copy-start.2) | copy-done | bytes 196632
  3.2 15.3 %shard_map.64.field_ref = f32[16,16,384]{2,1,0:T(8,128)S(1)} custom-call(f32[2,2,12288]{2,1,0:T(2,128)S(1)} %copy-done.2, s32[64,192]{1,0:T(8,128)S(1)} %fusion.pw_ref, bf16[8,256,256]{2,1,0:T(8,128)(2,1)S(1)} %copy-done.1), custom_call_target="tpu_custom_call" | custom-call | bytes 39321600 | tf_op jit(solution)/shard_map/pallas_call | solution.py:437
  18.5 0.0 copy-done.3
  18.5 13.9 %shard_map.65.grid_ref = f32[4096,128]{1,0:T(8,128)S(1)} custom-call(s32[3072]{0:T(1024)S(1)} %copy-done.3, f32[16,16,384]{2,1,0:T(8,128)S(1)} %shard_map.64.field_ref, f32[1024,128]{1,0:T(8,128)S(1)} %bitcast.9, bf16[8,256,256]{2,1,0:T(8,128)(2,1)S(1)} %copy-done.1), custom_call_target="tpu_custom_call" | custom-call | bytes 39321600 | tf_op jit(solution)/shard_map/pallas_call | solution.py:453
  32.4 0.1 constant_dynamic-slice_fusion
  32.5 0.1 copy.8
  32.6 0.1 reshape.18.pw_ref
  32.7 0.1 reshape.15
  32.8 14.4 %shard_map.66 = f32[2,2,96,128]{3,2,1,0:T(8,128)S(1)} custom-call(s32[3072]{0:T(1024)S(1)} %copy-done.3, s32[16,1,256]{2,1,0:T(1,128)S(1)} %pad.4.slot_ref, f32[4096,128]{1,0:T(8,128)S(1)} %shard_map.65.grid_ref, s32[96,128]{1,0:T(8,128)S(1)} %reshape.18.pw_ref, bf16[8,256,256]{2,1,0:T(8,128)(2,1)S(1)} %copy-done.1), custom_call_target="tpu_custom_call" | custom-call | bytes 39321600 | tf_op jit(solution)/shard_map/pallas_call | solution.py:467
  47.2 0.8 %reshape.19 = f32[2,2,12288]{2,1,0:T(2,128)} reshape(f32[2,2,96,128]{3,2,1,0:T(8,128)S(1)} %shard_map.66) | data formatting | bytes 393216 | tf_op jit(solution)/shard_map/reshape | solution.py:484
  (1 shorter events, 0.0 us)
Async XLA Ops:
  0.0 0.9 %copy-start = (s32[384,64]{0,1:T(8,128)S(1)}, s32[384,64]{0,1:T(8,128)}, u32[]{:S(2)}) copy-start(s32[384,64]{0,1:T(8,128)} %param.8) | copy-start | bytes 294916
  0.0 2.2 %copy-start.1 = (bf16[8,256,256]{2,1,0:T(8,128)(2,1)S(1)}, bf16[8,256,256]{2,1,0:T(8,128)(2,1)}, u32[]{:S(2)}) copy-start(bf16[8,256,256]{2,1,0:T(8,128)(2,1)} %constant.16.clone.table_ref) | copy-start | bytes 3145732
  0.0 18.5 %copy-start.3 = (s32[3072]{0:T(1024)S(1)}, s32[3072]{0:T(1024)}, u32[]{:S(2)}) copy-start(s32[3072]{0:T(1024)} %cols_ref.3) | copy-start | bytes 36868
  2.3 0.9 %copy-start.2 = (f32[2,2,12288]{2,1,0:T(2,128)S(1)}, f32[2,2,12288]{2,1,0:T(2,128)}, u32[]{:S(2)}) copy-start(f32[2,2,12288]{2,1,0:T(2,128)} %coeff_ref.1) | copy-start | bytes 589828

commit v3 on v2

--- a/solution.py
+++ b/solution.py
@@ -228,25 +228,17 @@
 
     lane = lax.broadcasted_iota(jnp.int32, (1, LANES), 1)
     first_of_lane = (lane // bz % slots) * group_rows
-    group = GROUP // 2
-
-    def fetch(step):
+    group = math.gcd(total, 3 * GROUP // 2)
+
+    @pl.loop(0, total // group)
+    def _(step):
         base = pl.multiple_of(step * group, group)
         cols = [cols_ref[base + i] for i in range(group)]
-        return cols, [sticks[pl.ds(base + i, 1), :] for i in range(group)]
-
-    def scatter(cols, values):
+        values = [sticks[pl.ds(base + i, 1), :] for i in range(group)]
         for col, value in zip(cols, values):
             spread = jnp.full((1, LANES), col, jnp.int32)
             mask = (spread & -group_rows) == first_of_lane
             pltpu.store(grid.at[pl.ds(col & (group_rows - 1), 1), :], value, mask=mask)
-
-    def each(step, held):
-        following = fetch(step)
-        scatter(*held)
-        return following
-
-    scatter(*lax.fori_loop(1, total // group, each, fetch(0)))
 
     @pl.loop(0, inner // batch)
     def _(step):

time: 48.1 us -> 45.8 us (0.952)
  Pallas kernels: 43.6 us -> 41.2 us
    pallas_call x1, Pallas kernels: 13.9 us -> 11.5 us  [local(): pl.pallas_call(partial(plane_kernel, bands), out_shape=jax.ShapeDtypeStru...]
where the time goes in v3:
time: 45.8 us; the launch traced here: 45.6 us
  Pallas kernels  41.2 us (90%)
  local copies, waits for them, and re-layouts  3.06 us (7%)
  other arithmetic  1.26 us (3%)
    pallas_call x1, Pallas kernels, local(): pl.pallas_call(depth_up, out_shape=jax.ShapeDtypeStruct(block, F32), in_s...  15.3 us
    pallas_call x1, Pallas kernels, local(): pl.pallas_call(depth_down, out_shape=jax.ShapeDtypeStruct(coeff, F32), in...  14.4 us
    pallas_call x1, Pallas kernels, local(): pl.pallas_call(partial(plane_kernel, bands), out_shape=jax.ShapeDtypeStru...  11.5 us
    unnamed x8, local copies, waits for them, and re-layouts  1.82 us
    transpose x1, other arithmetic, local(): potential = potential.reshape(planes, length, length).transpose(1, 0, 2)  1.26 us

profile of v3, /device:TPU:0, one launch (start us, length us, event | category | flops | bytes accessed | tf_op | source)
XLA Modules:
  0.0 45.6 jit_solution(2467691209957409652)
XLA Ops:
  0.0 0.0 copy-start
  0.0 0.0 copy-start.1
  0.0 0.0 copy-start.3
  0.0 0.9 %copy-done = s32[384,64]{0,1:T(8,128)S(1)} copy-done((s32[384,64]{0,1:T(8,128)S(1)}, s32[384,64]{0,1:T(8,128)}, u32[]{:S(2)}) %copy-start) | copy-done | bytes 98328
  0.9 0.1 fusion.pw_ref
  1.0 1.3 %add_bitcast_fusion = f32[128,8,128]{2,1,0:T(8,128)S(1)} fusion(f32[16,16384]{1,0:T(8,128)} %param.10, s32[]{:T(128)S(6)} %select_n.9, f32[16,16384]{1,0:T(8,128)} %param.9), kind=kLoop, calls=%fused_computation | loop fusion | flops 131072 | bytes 1572868 | tf_op jit(solution)/shard_map/transpose | solution.py:418
  2.2 0.0 copy-done.1
  2.3 0.0 copy-start.2
  2.3 0.9 %copy-done.2 = f32[2,2,12288]{2,1,0:T(2,128)S(1)} copy-done((f32[2,2,12288]{2,1,0:T(2,128)S(1)}, f32[2,2,12288]{2,1,0:T(2,128)}, u32[]{:S(2)}) %copy-start.2) | copy-done | bytes 196632
  3.2 15.3 %shard_map.64.field_ref = f32[16,16,384]{2,1,0:T(8,128)S(1)} custom-call(f32[2,2,12288]{2,1,0:T(2,128)S(1)} %copy-done.2, s32[64,192]{1,0:T(8,128)S(1)} %fusion.pw_ref, bf16[8,256,256]{2,1,0:T(8,128)(2,1)S(1)} %copy-done.1), custom_call_target="tpu_custom_call" | custom-call | bytes 39321600 | tf_op jit(solution)/shard_map/pallas_call | solution.py:429
  18.5 0.0 copy-done.3
  18.5 11.5 %shard_map.65.grid_ref = f32[4096,128]{1,0:T(8,128)S(1)} custom-call(s32[3072]{0:T(1024)S(1)} %copy-done.3, f32[16,16,384]{2,1,0:T(8,128)S(1)} %shard_map.64.field_ref, f32[1024,128]{1,0:T(8,128)S(1)} %bitcast.9, bf16[8,256,256]{2,1,0:T(8,128)(2,1)S(1)} %copy-done.1), custom_call_target="tpu_custom_call" | custom-call | bytes 39321600 | tf_op jit(solution)/shard_map/pallas_call | solution.py:445
  30.0 0.1 constant_dynamic-slice_fusion
  30.1 0.1 copy.8
  30.2 0.1 reshape.18.pw_ref
  30.3 0.1 reshape.15
  30.4 14.4 %shard_map.66 = f32[2,2,96,128]{3,2,1,0:T(8,128)S(1)} custom-call(s32[3072]{0:T(1024)S(1)} %copy-done.3, s32[16,1,256]{2,1,0:T(1,128)S(1)} %pad.4.slot_ref, f32[4096,128]{1,0:T(8,128)S(1)} %shard_map.65.grid_ref, s32[96,128]{1,0:T(8,128)S(1)} %reshape.18.pw_ref, bf16[8,256,256]{2,1,0:T(8,128)(2,1)S(1)} %copy-done.1), custom_call_target="tpu_custom_call" | custom-call | bytes 39321600 | tf_op jit(solution)/shard_map/pallas_call | solution.py:459
  44.8 0.8 %reshape.19 = f32[2,2,12288]{2,1,0:T(2,128)} reshape(f32[2,2,96,128]{3,2,1,0:T(8,128)S(1)} %shard_map.66) | data formatting | bytes 393216 | tf_op jit(solution)/shard_map/reshape | solution.py:476
  (1 shorter events, 0.0 us)
Async XLA Ops:
  0.0 0.9 %copy-start = (s32[384,64]{0,1:T(8,128)S(1)}, s32[384,64]{0,1:T(8,128)}, u32[]{:S(2)}) copy-start(s32[384,64]{0,1:T(8,128)} %param.8) | copy-start | bytes 294916
  0.0 2.2 %copy-start.1 = (bf16[8,256,256]{2,1,0:T(8,128)(2,1)S(1)}, bf16[8,256,256]{2,1,0:T(8,128)(2,1)}, u32[]{:S(2)}) copy-start(bf16[8,256,256]{2,1,0:T(8,128)(2,1)} %constant.16.clone.table_ref) | copy-start | bytes 3145732
  0.0 18.5 %copy-start.3 = (s32[3072]{0:T(1024)S(1)}, s32[3072]{0:T(1024)}, u32[]{:S(2)}) copy-start(s32[3072]{0:T(1024)} %cols_ref.3) | copy-start | bytes 36868
  2.3 0.9 %copy-start.2 = (f32[2,2,12288]{2,1,0:T(2,128)S(1)}, f32[2,2,12288]{2,1,0:T(2,128)}, u32[]{:S(2)}) copy-start(f32[2,2,12288]{2,1,0:T(2,128)} %coeff_ref.1) | copy-start | bytes 589828

commit v4 on v3

--- a/solution.py
+++ b/solution.py
@@ -404,6 +404,10 @@
     bz = bands * planes
     slots = LANES // (2 * bz)
 
+    potential = lax.dynamic_slice_in_dim(v_local, core * planes, planes, 0)
+    potential = potential + lax.dynamic_slice_in_dim(dv, core * planes, planes, 0)
+    potential = potential.reshape(planes, length, length).transpose(1, 0, 2)
+    pw_z, potential = lax.optimization_barrier((pw_z, potential))
     rows = lax.dynamic_slice_in_dim(pw_z, core * own, own, 0).reshape(pairs, 2 * zpw)
     coeff = (2, bands, pairs, 2 * zpw)
     by_wave = lax.dynamic_slice_in_dim(pw_z.T, core * own, own, 1)
@@ -413,10 +417,6 @@
     tables += [np.concatenate(halves(table), axis=1) for table in row_tables(length)]
     tables += halves(column) + halves(np.ascontiguousarray(column.T))
     tables = jnp.asarray(np.stack(tables))
-    potential = lax.dynamic_slice_in_dim(v_local, core * planes, planes, 0)
-    potential = potential + lax.dynamic_slice_in_dim(dv, core * planes, planes, 0)
-    potential = potential.reshape(planes, length, length).transpose(1, 0, 2)
-    by_wave, potential = lax.optimization_barrier((by_wave, potential))
     potential = potential.reshape(length * planes, length)
 
     slot_cols = jnp.pad(stick_cols.reshape(devices, 1, own), ((0, 0), (0, 0), (0, -own % LANES)))

time: 45.8 us -> 45.9 us (level)
  other arithmetic: 1.26 us -> 2.14 us
  local copies, waits for them, and re-layouts: 3.06 us -> 2.23 us
    transpose x1, other arithmetic: 1.26 us -> 2.14 us  [local(): potential = potential.reshape(planes, length, length).transpose(1, 0, 2)]
    unnamed x8 -> x10, local copies, waits for them, and re-layouts: 1.82 us -> 0.99 us
where the time goes in v4:
time: 45.9 us; the launch traced here: 45.7 us
  Pallas kernels  41.2 us (90%)
  local copies, waits for them, and re-layouts  2.23 us (5%)
  other arithmetic  2.14 us (5%)
    pallas_call x1, Pallas kernels, local(): pl.pallas_call(depth_up, out_shape=jax.ShapeDtypeStruct(block, F32), in_s...  15.3 us
    pallas_call x1, Pallas kernels, local(): pl.pallas_call(depth_down, out_shape=jax.ShapeDtypeStruct(coeff, F32), in...  14.4 us
    pallas_call x1, Pallas kernels, local(): pl.pallas_call(partial(plane_kernel, bands), out_shape=jax.ShapeDtypeStru...  11.5 us
    transpose x1, other arithmetic, local(): potential = potential.reshape(planes, length, length).transpose(1, 0, 2)  2.14 us
    unnamed x10, local copies, waits for them, and re-layouts  0.99 us

profile of v4, /device:TPU:0, one launch (start us, length us, event | category | flops | bytes accessed | tf_op | source)
XLA Modules:
  0.0 45.7 jit_solution(13666016207387367207)
XLA Ops:
  0.0 0.0 copy-start
  0.0 0.0 copy-start.1
  0.0 0.0 copy-start.4
  0.0 2.1 %add_bitcast_fusion = f32[128,8,128]{2,1,0:T(8,128)} fusion(f32[16,16384]{1,0:T(8,128)} %param.10, s32[]{:T(128)S(6)} %select_n.8, f32[16,16384]{1,0:T(8,128)} %param.9), kind=kLoop, calls=%fused_computation | loop fusion | flops 131072 | bytes 1572868 | tf_op jit(solution)/shard_map/transpose | solution.py:409
  2.2 0.0 copy-done
  2.2 0.0 copy-start.2
  2.2 0.1 fusion.pw_ref
  2.2 0.0 copy-done.1
  2.3 0.0 copy-start.3
  2.3 1.0 %copy-done.3 = f32[2,2,12288]{2,1,0:T(2,128)S(1)} copy-done((f32[2,2,12288]{2,1,0:T(2,128)S(1)}, f32[2,2,12288]{2,1,0:T(2,128)}, u32[]{:S(2)}) %copy-start.3) | copy-done | bytes 196632
  3.2 15.3 %shard_map.64.field_ref = f32[16,16,384]{2,1,0:T(8,128)S(1)} custom-call(f32[2,2,12288]{2,1,0:T(2,128)S(1)} %copy-done.3, s32[64,192]{1,0:T(8,128)S(1)} %fusion.pw_ref, bf16[8,256,256]{2,1,0:T(8,128)(2,1)S(1)} %copy-done.1), custom_call_target="tpu_custom_call" | custom-call | bytes 39321600 | tf_op jit(solution)/shard_map/pallas_call | solution.py:429
  18.6 0.0 copy-done.4
  18.6 0.0 copy-done.2
  18.6 11.5 %shard_map.65.grid_ref = f32[4096,128]{1,0:T(8,128)S(1)} custom-call(s32[3072]{0:T(1024)S(1)} %copy-done.4, f32[16,16,384]{2,1,0:T(8,128)S(1)} %shard_map.64.field_ref, f32[1024,128]{1,0:T(8,128)S(1)} %bitcast.9, bf16[8,256,256]{2,1,0:T(8,128)(2,1)S(1)} %copy-done.1), custom_call_target="tpu_custom_call" | custom-call | bytes 39321600 | tf_op jit(solution)/shard_map/pallas_call | solution.py:445
  30.1 0.1 constant_dynamic-slice_fusion
  30.2 0.1 copy.8
  30.3 0.1 reshape.18.pw_ref
  30.4 0.1 reshape.15
  30.5 14.4 %shard_map.66 = f32[2,2,96,128]{3,2,1,0:T(8,128)S(1)} custom-call(s32[3072]{0:T(1024)S(1)} %copy-done.4, s32[16,1,256]{2,1,0:T(1,128)S(1)} %pad.4.slot_ref, f32[4096,128]{1,0:T(8,128)S(1)} %shard_map.65.grid_ref, s32[96,128]{1,0:T(8,128)S(1)} %reshape.18.pw_ref, bf16[8,256,256]{2,1,0:T(8,128)(2,1)S(1)} %copy-done.1), custom_call_target="tpu_custom_call" | custom-call | bytes 39321600 | tf_op jit(solution)/shard_map/pallas_call | solution.py:459
  44.9 0.8 %reshape.19 = f32[2,2,12288]{2,1,0:T(2,128)} reshape(f32[2,2,96,128]{3,2,1,0:T(8,128)S(1)} %shard_map.66) | data formatting | bytes 393216 | tf_op jit(solution)/shard_map/reshape | solution.py:476
  (1 shorter events, 0.0 us)
Async XLA Ops:
  0.0 2.2 %copy-start = (s32[384,64]{0,1:T(8,128)S(1)}, s32[384,64]{0,1:T(8,128)}, u32[]{:S(2)}) copy-start(s32[384,64]{0,1:T(8,128)} %param.8) | copy-start | bytes 294916
  0.0 2.2 %copy-start.1 = (bf16[8,256,256]{2,1,0:T(8,128)(2,1)S(1)}, bf16[8,256,256]{2,1,0:T(8,128)(2,1)}, u32[]{:S(2)}) copy-start(bf16[8,256,256]{2,1,0:T(8,128)(2,1)} %constant.16.clone.table_ref) | copy-start | bytes 3145732
  0.0 18.6 %copy-start.4 = (s32[3072]{0:T(1024)S(1)}, s32[3072]{0:T(1024)}, u32[]{:S(2)}) copy-start(s32[3072]{0:T(1024)} %cols_ref.3) | copy-start | bytes 36868
  2.2 16.4 %copy-start.2 = (f32[128,8,128]{2,1,0:T(8,128)S(1)}, f32[128,8,128]{2,1,0:T(8,128)}, u32[]{:S(2)}) copy-start(f32[128,8,128]{2,1,0:T(8,128)} %add_bitcast_fusion) | copy-start | bytes 1572868
  2.3 1.0 %copy-start.3 = (f32[2,2,12288]{2,1,0:T(2,128)S(1)}, f32[2,2,12288]{2,1,0:T(2,128)}, u32[]{:S(2)}) copy-start(f32[2,2,12288]{2,1,0:T(2,128)} %coeff_ref.1) | copy-start | bytes 589828
